TPU v7x, 256 devices: a whole 4x4x8 slice. The times are simulated.
256 devices in a mesh: lat: 32 (over z, y_lo, core), lon: 8 (over x, y_hi).
Axes of the slice: x: 4, y: 4 (y_hi: 2, y_lo: 2; y = y_hi * 2 + y_lo), z: 8, core: 2. Of those that a mesh axis runs over, the one named last changes fastest.
Arguments:
- increment: float32 [2, 6, 768, 4096], P(None, None, 'lat', 'lon'), may hold values from -6 to 6
- normal_gain: float32 [2, 6, 768, 4096], P(None, None, 'lat', 'lon'), may hold values from 0.5 to 2
- coef_x: float32 [6, 768, 4096], P(None, 'lat', 'lon'), may hold values from 0.08 to 0.12
- coef_y: float32 [6, 768, 4096], P(None, 'lat', 'lon'), may hold values from 0.08 to 0.12
- ocean: int32 [6, 768, 4096], P(None, 'lat', 'lon'), may hold values 0 or 1
- inv_area: float32 [768, 4096], P('lat', 'lon'), may hold values from 1.6 to 2
- partner: int32 [4096], replicated, may hold values from 0 to 4095, as said below
Outputs:
- adjoint_field: float32 [2, 6, 768, 4096], P(None, None, 'lat', 'lon')
Inputs may be any that keep to these rules, and one draw needn't show every extreme that they name: partner[i] = (c - i) mod 4096 for one c drawn per draw, so partner[partner[i]] = i.
All inputs are finite; a program needn't handle non-finite values. No bound on the sum of `ocean` on one device may be relied on, other than what follows from the above.
Results may differ from a plain program's by a relative error of at most 0.00002.
Values sent between devices are 32-bit elements; how exact they have to be, the bound alone decides.
A program may use at most 64 MiB of HBM per device.

v0:
```python
import jax
import jax.numpy as jnp
from jax import lax
from jax.sharding import PartitionSpec as P

ITERS = 10


def padded(cells, sides, width):
    for axis, dim in sides:
        count = lax.axis_size(axis)
        head = lax.slice_in_dim(cells, 0, width, axis=dim)
        tail = lax.slice_in_dim(cells, cells.shape[dim] - width, cells.shape[dim], axis=dim)
        cells = jnp.concatenate(
            [
                lax.ppermute(tail, axis, [(i, (i + 1) % count) for i in range(count)]),
                cells,
                lax.ppermute(head, axis, [((i + 1) % count, i) for i in range(count)]),
            ],
            axis=dim,
        )
    return cells


def widen(field, width):
    return padded(field, (("lat", 2), ("lon", 3)), width)


def on_device(increment, normal_gain, coef_x, coef_y, ocean, inv_area, partner):
    levels, rows, cols = coef_x.shape
    n_lat = lax.axis_size("lat")
    n_lon = lax.axis_size("lon")
    lat_pos = lax.axis_index("lat")
    lon_pos = lax.axis_index("lon")
    total_rows = rows * n_lat
    total_cols = cols * n_lon
    oceanf = ocean.astype(jnp.float32)
    stacked = jnp.concatenate([coef_x, coef_y, oceanf, inv_area[None]], axis=0)
    framed = padded(stacked, (("lat", 1), ("lon", 2)), 2)
    kx_frame = framed[:levels]
    ky_frame = framed[levels : 2 * levels]
    mask_frame = framed[2 * levels : 3 * levels]
    area_frame = framed[3 * levels]
    global_rows = lat_pos * rows + jnp.arange(rows + 4, dtype=jnp.int32) - 2
    global_cols = jnp.mod(lon_pos * cols + jnp.arange(cols + 4, dtype=jnp.int32) - 2, total_cols)
    ex_frame = kx_frame[:, :, :-1] * mask_frame[:, :, :-1] * mask_frame[:, :, 1:]
    link_rows = global_rows[:-1]
    valid_link = (link_rows >= 0) & (link_rows < total_rows - 1)
    ey_frame = jnp.where(
        valid_link[None, :, None], ky_frame[:, :-1] * mask_frame[:, :-1] * mask_frame[:, 1:], 0.0
    )
    top_local = jnp.concatenate([coef_y[:, -1], oceanf[:, -1], inv_area[-1][None]], axis=0)
    top_full = lax.all_gather(top_local, "lon", axis=1, tiled=True)
    mirror = jnp.take(partner, global_cols)
    top_coef = top_full[:levels]
    top_mask = top_full[levels : 2 * levels]
    top_area = top_full[2 * levels]
    ef_frame = (
        0.5
        * (jnp.take(top_coef, global_cols, axis=1) + jnp.take(top_coef, mirror, axis=1))
        * jnp.take(top_mask, global_cols, axis=1)
        * jnp.take(top_mask, mirror, axis=1)
    )
    is_top = lat_pos == n_lat - 1
    ef_frame = jnp.where(is_top, ef_frame, 0.0)
    mirror_area = jnp.take(top_area, mirror)
    field = normal_gain * oceanf * increment
    for step in range(ITERS):
        advance_field = widen(field, 1)
        start = 2 - 1
        height = rows + 2 * 1
        width = cols + 2 * 1
        ex_now = ex_frame[:, start : start + height, start : start + width - 1]
        ey_now = ey_frame[:, start : start + height - 1, start : start + width]
        area_now = area_frame[start : start + height, start : start + width]
        ef_now = ef_frame[:, start : start + width]
        mirror_now = mirror[start : start + width]
        area_mirror = mirror_area[start : start + width]
        top_row = rows - 1 + 1
        own_row = advance_field[:, :, top_row, 1 : 1 + cols]
        whole_row = lax.all_gather(own_row, "lon", axis=2, tiled=True)
        scaled = area_now * advance_field
        partner_scaled = area_mirror * jnp.take(whole_row, mirror_now, axis=2)
        centre = scaled[:, :, 1:-1, 1:-1]
        right = scaled[:, :, 1:-1, 2:]
        left = scaled[:, :, 1:-1, :-2]
        upper = scaled[:, :, 2:, 1:-1]
        lower = scaled[:, :, :-2, 1:-1]
        delta = ex_now[:, 1:-1, 1:] * (right - centre) + ex_now[:, 1:-1, :-1] * (left - centre)
        delta = (
            delta + ey_now[:, 1:, 1:-1] * (upper - centre) + ey_now[:, :-1, 1:-1] * (lower - centre)
        )
        fold_term = ef_now[:, 1:-1] * (partner_scaled[:, :, 1:-1] - scaled[:, :, top_row, 1:-1])
        row_pick = jnp.arange(height - 2, dtype=jnp.int32) == top_row - 1
        delta = delta + jnp.where(row_pick[:, None], fold_term[:, :, None, :], 0.0)
        field = advance_field[:, :, 1:-1, 1:-1] + delta
    return field


def solution(mesh):
    in_specs = (
        P(None, None, "lat", "lon"),
        P(None, None, "lat", "lon"),
        P(None, "lat", "lon"),
        P(None, "lat", "lon"),
        P(None, "lat", "lon"),
        P("lat", "lon"),
        P(),
    )
    out_specs = P(None, None, "lat", "lon")
    return jax.shard_map(
        on_device, mesh=mesh, in_specs=in_specs, out_specs=out_specs, check_vma=False
    )
```

profile of v0, /device:TPU:225, one launch (start us, length us, event | category | flops | bytes accessed | tf_op | source)
XLA Modules:
  0.0 774.8 jit_solution(3107213091279716373)
XLA Ops:
  13.2 45.8 %all_gather.33 = f32[13,4096]{0,1:T(8,128)S(1)} all-gather(f32[13,512]{0,1:T(8,128)S(1)} %copy.1127), channel_id=1, replica_groups=mesh['lat'=32,'lon'=8] {'lon'}, dimensions={1}, use_global_device_ids=true | all-gather | bytes 239616 | tf_op jit(solution)/shard_map/all_gather | solution.py:53
  78.8 28.3 %all-gather = f32[2,6,1,4096]{3,0,2,1:T(2,128)S(1)} all-gather(f32[2,6,1,512]{3,0,2,1:T(2,128)S(1)} %copy.1128), channel_id=2, replica_groups=mesh['lat'=32,'lon'=8] {'lon'}, dimensions={3}, use_global_device_ids=true | all-gather | bytes 221184 | tf_op jit(solution)/shard_map/all_gather | solution.py:81
  120.9 5.1 collective-permute-start.7
  149.0 12.2 %collective-permute-start.8 = (f32[2,6,1,512]{3,2,1,0:T(1,128)S(1)}, f32[2,6,1,512]{3,2,1,0:T(1,128)S(1)}, u32[]{:S(2)}, u32[]{:S(2)}) collective-permute-start(f32[2,6,1,512]{3,2,1,0:T(1,128)S(1)} %get-tuple-element.54), channel_id=1, source_target_pairs={{0,8},{8,16},{16,24},{24,32},{32,40},{40,48},{48,56},{56,64},{64,7... | collective-permute-start | bytes 73736 | tf_op jit(solution)/shard_map/ppermute | solution.py:16
  161.3 27.9 %all-gather.1 = f32[2,6,1,4096]{3,0,2,1:T(2,128)S(1)} all-gather(f32[2,6,1,512]{3,0,2,1:T(2,128)S(1)} %copy.1137), channel_id=3, replica_groups=mesh['lat'=32,'lon'=8] {'lon'}, dimensions={3}, use_global_device_ids=true | all-gather | bytes 221184 | tf_op jit(solution)/shard_map/all_gather | solution.py:81
  197.3 8.6 %collective-permute-start.9 = (f32[2,6,1,512]{3,2,1,0:T(1,128)S(1)}, f32[2,6,1,512]{3,2,1,0:T(1,128)S(1)}, u32[]{:S(2)}, u32[]{:S(2)}) collective-permute-start(f32[2,6,1,512]{3,2,1,0:T(1,128)S(1)} %get-tuple-element.53), channel_id=1, source_target_pairs={{8,0},{16,8},{24,16},{32,24},{40,32},{48,40},{56,48},{64,56},{72,6... | collective-permute-start | bytes 73736 | tf_op jit(solution)/shard_map/ppermute | solution.py:18
  231.7 27.9 %all-gather.2 = f32[2,6,1,4096]{3,0,2,1:T(2,128)S(1)} all-gather(f32[2,6,1,512]{3,0,2,1:T(2,128)S(1)} %copy.1146), channel_id=4, replica_groups=mesh['lat'=32,'lon'=8] {'lon'}, dimensions={3}, use_global_device_ids=true | all-gather | bytes 221184 | tf_op jit(solution)/shard_map/all_gather | solution.py:81
  267.7 6.9 collective-permute-start.13
  278.5 5.2 collective-permute-start.15
  298.9 28.2 %all-gather.3 = f32[2,6,1,4096]{3,0,2,1:T(2,128)S(1)} all-gather(f32[2,6,1,512]{3,0,2,1:T(2,128)S(1)} %copy.1155), channel_id=5, replica_groups=mesh['lat'=32,'lon'=8] {'lon'}, dimensions={3}, use_global_device_ids=true | all-gather | bytes 221184 | tf_op jit(solution)/shard_map/all_gather | solution.py:81
  335.2 7.2 collective-permute-start.17
  367.3 27.9 %all-gather.4 = f32[2,6,1,4096]{3,0,2,1:T(2,128)S(1)} all-gather(f32[2,6,1,512]{3,0,2,1:T(2,128)S(1)} %copy.1164), channel_id=6, replica_groups=mesh['lat'=32,'lon'=8] {'lon'}, dimensions={3}, use_global_device_ids=true | all-gather | bytes 221184 | tf_op jit(solution)/shard_map/all_gather | solution.py:81
  403.3 7.4 collective-permute-start.21
  414.7 5.2 collective-permute-start.23
  435.3 28.1 %all-gather.5 = f32[2,6,1,4096]{3,0,2,1:T(2,128)S(1)} all-gather(f32[2,6,1,512]{3,0,2,1:T(2,128)S(1)} %copy.1173), channel_id=7, replica_groups=mesh['lat'=32,'lon'=8] {'lon'}, dimensions={3}, use_global_device_ids=true | all-gather | bytes 221184 | tf_op jit(solution)/shard_map/all_gather | solution.py:81
  471.4 7.2 collective-permute-start.25
  504.0 28.4 %all-gather.6 = f32[2,6,1,4096]{3,0,2,1:T(2,128)S(1)} all-gather(f32[2,6,1,512]{3,0,2,1:T(2,128)S(1)} %copy.1182), channel_id=8, replica_groups=mesh['lat'=32,'lon'=8] {'lon'}, dimensions={3}, use_global_device_ids=true | all-gather | bytes 221184 | tf_op jit(solution)/shard_map/all_gather | solution.py:81
  540.5 6.8 collective-permute-start.29
  571.7 28.0 %all-gather.7 = f32[2,6,1,4096]{3,0,2,1:T(2,128)S(1)} all-gather(f32[2,6,1,512]{3,0,2,1:T(2,128)S(1)} %copy.1191), channel_id=9, replica_groups=mesh['lat'=32,'lon'=8] {'lon'}, dimensions={3}, use_global_device_ids=true | all-gather | bytes 221184 | tf_op jit(solution)/shard_map/all_gather | solution.py:81
  607.8 7.3 collective-permute-start.33
  640.1 28.3 %all-gather.8 = f32[2,6,1,4096]{3,0,2,1:T(2,128)S(1)} all-gather(f32[2,6,1,512]{3,0,2,1:T(2,128)S(1)} %copy.1200), channel_id=10, replica_groups=mesh['lat'=32,'lon'=8] {'lon'}, dimensions={3}, use_global_device_ids=true | all-gather | bytes 221184 | tf_op jit(solution)/shard_map/all_gather | solution.py:81
  676.5 6.8 collective-permute-start.37
  708.0 28.1 %all-gather.9 = f32[2,6,1,4096]{3,0,2,1:T(2,128)S(1)} all-gather(f32[2,6,1,512]{3,0,2,1:T(2,128)S(1)} %copy.1209), channel_id=11, replica_groups=mesh['lat'=32,'lon'=8] {'lon'}, dimensions={3}, use_global_device_ids=true | all-gather | bytes 221184 | tf_op jit(solution)/shard_map/all_gather | solution.py:81
  744.2 6.4 collective-permute-start.41
  (315 shorter events, 353.9 us)
Async XLA Ops:
  2.8 123.2 %collective-permute-start = (f32[19,2,512]{2,1,0:T(2,128)}, f32[19,2,512]{2,1,0:T(2,128)}, u32[]{:S(2)}, u32[]{:S(2)}) collective-permute-start(f32[19,2,512]{2,1,0:T(2,128)} %get-tuple-element.15), channel_id=1, source_target_pairs={{0,8},{8,16},{16,24},{24,32},{32,40},{40,48},{48,56},{56,64},{64,7... | collective-permute-start | bytes 233480 | tf_op jit(solution)/shard_map/ppermute | solution.py:16
  4.7 121.3 %collective-permute-start.1 = (f32[19,2,512]{2,1,0:T(2,128)}, f32[19,2,512]{2,1,0:T(2,128)}, u32[]{:S(2)}, u32[]{:S(2)}) collective-permute-start(f32[19,2,512]{2,1,0:T(2,128)} %get-tuple-element.16), channel_id=1, source_target_pairs={{8,0},{16,8},{24,16},{32,24},{40,32},{48,40},{56,48},{64,56},{72,6... | collective-permute-start | bytes 233480 | tf_op jit(solution)/shard_map/ppermute | solution.py:18
  6.8 111.5 %collective-permute-start.4 = (f32[2,6,1,512]{3,2,1,0:T(1,128)}, f32[2,6,1,512]{3,2,1,0:T(1,128)}, u32[]{:S(2)}, u32[]{:S(2)}) collective-permute-start(f32[2,6,1,512]{3,2,1,0:T(1,128)} %get-tuple-element.56), channel_id=1, source_target_pairs={{0,8},{8,16},{16,24},{24,32},{32,40},{40,48},{48,56},{56,64},{64,7... | collective-permute-start | bytes 73736 | tf_op jit(solution)/shard_map/ppermute | solution.py:16
  8.6 111.1 %collective-permute-start.5 = (f32[2,6,1,512]{3,2,1,0:T(1,128)}, f32[2,6,1,512]{3,2,1,0:T(1,128)}, u32[]{:S(2)}, u32[]{:S(2)}) collective-permute-start(f32[2,6,1,512]{3,2,1,0:T(1,128)} %get-tuple-element.55), channel_id=1, source_target_pairs={{8,0},{16,8},{24,16},{32,24},{40,32},{48,40},{56,48},{64,56},{72,6... | collective-permute-start | bytes 73736 | tf_op jit(solution)/shard_map/ppermute | solution.py:18
  120.7 11.5 %collective-permute-start.6 = (f32[2,6,26,1]{3,0,2,1:T(2,128)S(1)}, f32[2,6,26,1]{3,0,2,1:T(2,128)S(1)}, u32[]{:S(2)}, u32[]{:S(2)}) collective-permute-start(f32[2,6,26,1]{3,0,2,1:T(2,128)S(1)} %get-tuple-element.35), channel_id=1, source_target_pairs={{0,1},{1,2},{2,3},{3,4},{4,5},{5,6},{6,7},{7,0},{8,9},{9,10},{10,1... | collective-permute-start | bytes 3752 | tf_op jit(solution)/shard_map/ppermute | solution.py:16
  120.9 11.3 %collective-permute-start.7 = (f32[2,6,26,1]{3,0,2,1:T(2,128)S(1)}, f32[2,6,26,1]{3,0,2,1:T(2,128)S(1)}, u32[]{:S(2)}, u32[]{:S(2)}) collective-permute-start(f32[2,6,26,1]{3,0,2,1:T(2,128)S(1)} %get-tuple-element.36), channel_id=1, source_target_pairs={{1,0},{2,1},{3,2},{4,3},{5,4},{6,5},{7,6},{0,7},{9,8},{10,9},{11,1... | collective-permute-start | bytes 3752 | tf_op jit(solution)/shard_map/ppermute | solution.py:18
  127.1 10.7 %collective-permute-start.3 = (f32[19,28,2]{2,1,0:T(8,128)S(1)}, f32[19,28,2]{2,1,0:T(8,128)S(1)}, u32[]{:S(2)}, u32[]{:S(2)}) collective-permute-start(f32[19,28,2]{2,1,0:T(8,128)S(1)} %get-tuple-element.14), channel_id=1, source_target_pairs={{1,0},{2,1},{3,2},{4,3},{5,4},{6,5},{7,6},{0,7},{9,8},{10,9},{11,1... | collective-permute-start | bytes 12776 | tf_op jit(solution)/shard_map/ppermute | solution.py:18
  149.0 56.8 %collective-permute-start.8 = (f32[2,6,1,512]{3,2,1,0:T(1,128)S(1)}, f32[2,6,1,512]{3,2,1,0:T(1,128)S(1)}, u32[]{:S(2)}, u32[]{:S(2)}) collective-permute-start(f32[2,6,1,512]{3,2,1,0:T(1,128)S(1)} %get-tuple-element.54), channel_id=1, source_target_pairs={{0,8},{8,16},{16,24},{24,32},{32,40},{40,48},{48,56},{56,64},{64,7... | collective-permute-start | bytes 73736 | tf_op jit(solution)/shard_map/ppermute | solution.py:16
  211.6 11.2 %collective-permute-start.11 = (f32[2,6,26,1]{3,0,2,1:T(2,128)S(1)}, f32[2,6,26,1]{3,0,2,1:T(2,128)S(1)}, u32[]{:S(2)}, u32[]{:S(2)}) collective-permute-start(f32[2,6,26,1]{3,0,2,1:T(2,128)S(1)} %get-tuple-element.34), channel_id=1, source_target_pairs={{1,0},{2,1},{3,2},{4,3},{5,4},{6,5},{7,6},{0,7},{9,8},{10,9},{11,1... | collective-permute-start | bytes 3752 | tf_op jit(solution)/shard_map/ppermute | solution.py:18
  231.6 43.0 %collective-permute-start.12 = (f32[2,6,1,512]{3,2,1,0:T(1,128)S(1)}, f32[2,6,1,512]{3,2,1,0:T(1,128)S(1)}, u32[]{:S(2)}, u32[]{:S(2)}) collective-permute-start(f32[2,6,1,512]{3,2,1,0:T(1,128)S(1)} %get-tuple-element.52), channel_id=1, source_target_pairs={{0,8},{8,16},{16,24},{24,32},{32,40},{40,48},{48,56},{56,64},{64,7... | collective-permute-start | bytes 73736 | tf_op jit(solution)/shard_map/ppermute | solution.py:16
  278.5 10.7 %collective-permute-start.15 = (f32[2,6,26,1]{3,0,2,1:T(2,128)S(1)}, f32[2,6,26,1]{3,0,2,1:T(2,128)S(1)}, u32[]{:S(2)}, u32[]{:S(2)}) collective-permute-start(f32[2,6,26,1]{3,0,2,1:T(2,128)S(1)} %get-tuple-element.32), channel_id=1, source_target_pairs={{1,0},{2,1},{3,2},{4,3},{5,4},{6,5},{7,6},{0,7},{9,8},{10,9},{11,1... | collective-permute-start | bytes 3752 | tf_op jit(solution)/shard_map/ppermute | solution.py:18
  298.8 43.6 %collective-permute-start.16 = (f32[2,6,1,512]{3,2,1,0:T(1,128)S(1)}, f32[2,6,1,512]{3,2,1,0:T(1,128)S(1)}, u32[]{:S(2)}, u32[]{:S(2)}) collective-permute-start(f32[2,6,1,512]{3,2,1,0:T(1,128)S(1)} %get-tuple-element.50), channel_id=1, source_target_pairs={{0,8},{8,16},{16,24},{24,32},{32,40},{40,48},{48,56},{56,64},{64,7... | collective-permute-start | bytes 73736 | tf_op jit(solution)/shard_map/ppermute | solution.py:16
  347.7 10.7 %collective-permute-start.19 = (f32[2,6,26,1]{3,0,2,1:T(2,128)S(1)}, f32[2,6,26,1]{3,0,2,1:T(2,128)S(1)}, u32[]{:S(2)}, u32[]{:S(2)}) collective-permute-start(f32[2,6,26,1]{3,0,2,1:T(2,128)S(1)} %get-tuple-element.30), channel_id=1, source_target_pairs={{1,0},{2,1},{3,2},{4,3},{5,4},{6,5},{7,6},{0,7},{9,8},{10,9},{11,1... | collective-permute-start | bytes 3752 | tf_op jit(solution)/shard_map/ppermute | solution.py:18
  367.2 43.5 %collective-permute-start.20 = (f32[2,6,1,512]{3,2,1,0:T(1,128)S(1)}, f32[2,6,1,512]{3,2,1,0:T(1,128)S(1)}, u32[]{:S(2)}, u32[]{:S(2)}) collective-permute-start(f32[2,6,1,512]{3,2,1,0:T(1,128)S(1)} %get-tuple-element.48), channel_id=1, source_target_pairs={{0,8},{8,16},{16,24},{24,32},{32,40},{40,48},{48,56},{56,64},{64,7... | collective-permute-start | bytes 73736 | tf_op jit(solution)/shard_map/ppermute | solution.py:16
  414.7 10.6 %collective-permute-start.23 = (f32[2,6,26,1]{3,0,2,1:T(2,128)S(1)}, f32[2,6,26,1]{3,0,2,1:T(2,128)S(1)}, u32[]{:S(2)}, u32[]{:S(2)}) collective-permute-start(f32[2,6,26,1]{3,0,2,1:T(2,128)S(1)} %get-tuple-element.28), channel_id=1, source_target_pairs={{1,0},{2,1},{3,2},{4,3},{5,4},{6,5},{7,6},{0,7},{9,8},{10,9},{11,1... | collective-permute-start | bytes 3752 | tf_op jit(solution)/shard_map/ppermute | solution.py:18
  434.9 43.7 %collective-permute-start.24 = (f32[2,6,1,512]{3,2,1,0:T(1,128)S(1)}, f32[2,6,1,512]{3,2,1,0:T(1,128)S(1)}, u32[]{:S(2)}, u32[]{:S(2)}) collective-permute-start(f32[2,6,1,512]{3,2,1,0:T(1,128)S(1)} %get-tuple-element.46), channel_id=1, source_target_pairs={{0,8},{8,16},{16,24},{24,32},{32,40},{40,48},{48,56},{56,64},{64,7... | collective-permute-start | bytes 73736 | tf_op jit(solution)/shard_map/ppermute | solution.py:16
  483.9 11.2 %collective-permute-start.27 = (f32[2,6,26,1]{3,0,2,1:T(2,128)S(1)}, f32[2,6,26,1]{3,0,2,1:T(2,128)S(1)}, u32[]{:S(2)}, u32[]{:S(2)}) collective-permute-start(f32[2,6,26,1]{3,0,2,1:T(2,128)S(1)} %get-tuple-element.26), channel_id=1, source_target_pairs={{1,0},{2,1},{3,2},{4,3},{5,4},{6,5},{7,6},{0,7},{9,8},{10,9},{11,1... | collective-permute-start | bytes 3752 | tf_op jit(solution)/shard_map/ppermute | solution.py:18
  503.9 43.3 %collective-permute-start.28 = (f32[2,6,1,512]{3,2,1,0:T(1,128)S(1)}, f32[2,6,1,512]{3,2,1,0:T(1,128)S(1)}, u32[]{:S(2)}, u32[]{:S(2)}) collective-permute-start(f32[2,6,1,512]{3,2,1,0:T(1,128)S(1)} %get-tuple-element.44), channel_id=1, source_target_pairs={{0,8},{8,16},{16,24},{24,32},{32,40},{40,48},{48,56},{56,64},{64,7... | collective-permute-start | bytes 73736 | tf_op jit(solution)/shard_map/ppermute | solution.py:16
  571.4 43.7 %collective-permute-start.32 = (f32[2,6,1,512]{3,2,1,0:T(1,128)S(1)}, f32[2,6,1,512]{3,2,1,0:T(1,128)S(1)}, u32[]{:S(2)}, u32[]{:S(2)}) collective-permute-start(f32[2,6,1,512]{3,2,1,0:T(1,128)S(1)} %get-tuple-element.42), channel_id=1, source_target_pairs={{0,8},{8,16},{16,24},{24,32},{32,40},{40,48},{48,56},{56,64},{64,7... | collective-permute-start | bytes 73736 | tf_op jit(solution)/shard_map/ppermute | solution.py:16
  620.3 10.6 %collective-permute-start.35 = (f32[2,6,26,1]{3,0,2,1:T(2,128)S(1)}, f32[2,6,26,1]{3,0,2,1:T(2,128)S(1)}, u32[]{:S(2)}, u32[]{:S(2)}) collective-permute-start(f32[2,6,26,1]{3,0,2,1:T(2,128)S(1)} %get-tuple-element.22), channel_id=1, source_target_pairs={{1,0},{2,1},{3,2},{4,3},{5,4},{6,5},{7,6},{0,7},{9,8},{10,9},{11,1... | collective-permute-start | bytes 3752 | tf_op jit(solution)/shard_map/ppermute | solution.py:18
  639.8 43.6 %collective-permute-start.36 = (f32[2,6,1,512]{3,2,1,0:T(1,128)S(1)}, f32[2,6,1,512]{3,2,1,0:T(1,128)S(1)}, u32[]{:S(2)}, u32[]{:S(2)}) collective-permute-start(f32[2,6,1,512]{3,2,1,0:T(1,128)S(1)} %get-tuple-element.40), channel_id=1, source_target_pairs={{0,8},{8,16},{16,24},{24,32},{32,40},{40,48},{48,56},{56,64},{64,7... | collective-permute-start | bytes 73736 | tf_op jit(solution)/shard_map/ppermute | solution.py:16
  687.5 10.6 %collective-permute-start.39 = (f32[2,6,26,1]{3,0,2,1:T(2,128)S(1)}, f32[2,6,26,1]{3,0,2,1:T(2,128)S(1)}, u32[]{:S(2)}, u32[]{:S(2)}) collective-permute-start(f32[2,6,26,1]{3,0,2,1:T(2,128)S(1)} %get-tuple-element.20), channel_id=1, source_target_pairs={{1,0},{2,1},{3,2},{4,3},{5,4},{6,5},{7,6},{0,7},{9,8},{10,9},{11,1... | collective-permute-start | bytes 3752 | tf_op jit(solution)/shard_map/ppermute | solution.py:18
  706.9 43.7 %collective-permute-start.40 = (f32[2,6,1,512]{3,2,1,0:T(1,128)S(1)}, f32[2,6,1,512]{3,2,1,0:T(1,128)S(1)}, u32[]{:S(2)}, u32[]{:S(2)}) collective-permute-start(f32[2,6,1,512]{3,2,1,0:T(1,128)S(1)} %get-tuple-element.38), channel_id=1, source_target_pairs={{0,8},{8,16},{16,24},{24,32},{32,40},{40,48},{48,56},{56,64},{64,7... | collective-permute-start | bytes 73736 | tf_op jit(solution)/shard_map/ppermute | solution.py:16
  754.4 11.1 %collective-permute-start.43 = (f32[2,6,26,1]{3,0,2,1:T(2,128)S(1)}, f32[2,6,26,1]{3,0,2,1:T(2,128)S(1)}, u32[]{:S(2)}, u32[]{:S(2)}) collective-permute-start(f32[2,6,26,1]{3,0,2,1:T(2,128)S(1)} %get-tuple-element.18), channel_id=1, source_target_pairs={{1,0},{2,1},{3,2},{4,3},{5,4},{6,5},{7,6},{0,7},{9,8},{10,9},{11,1... | collective-permute-start | bytes 3752 | tf_op jit(solution)/shard_map/ppermute | solution.py:18
  (38 other events, 438.5 us)
where the time goes:
time: 789 us; the launch traced here: 775 us
  blocking collectives  327 us (41%)
  local copies, waits for them, and re-layouts  161 us (20%)
  starting transfers between devices  142 us (18%)
  other arithmetic  101 us (13%)
  waiting for transfers between devices  42.5 us (5%)
    all_gather x10, blocking collectives, on_device(): whole_row = lax.all_gather(own_row, 'lon', axis=2, tiled=True)  281 us
    ppermute x22, starting transfers between devices, padded(): lax.ppermute(head, axis, [((i + 1) % count, i) for i in range(count)])  114 us
    all_gather x1, blocking collectives, on_device(): top_full = lax.all_gather(top_local, 'lon', axis=1, tiled=True)  45.8 us
    all_gather x10, local copies, waits for them, and re-layouts, on_device(): whole_row = lax.all_gather(own_row, 'lon', axis=2, tiled=True)  43.7 us
    gather x10, local copies, waits for them, and re-layouts, on_device(): partner_scaled = area_mirror * jnp.take(whole_row, mirror_now, axis=2)  36.8 us
    mul x10, other arithmetic, on_device(): ef_now[:, 1:-1] * (partner_scaled[:, :, 1:-1] - scaled[:, :, top_row, 1:-1])  31.6 us
    ppermute x22, starting transfers between devices, padded(): lax.ppermute(tail, axis, [(i, (i + 1) % count) for i in range(count)])  28.2 us
    ppermute x22, waiting for transfers between devices, padded(): lax.ppermute(head, axis, [((i + 1) % count, i) for i in range(count)])  23.8 us
  transfers between devices with their start and end apart: 44, of which 21 were waited for; matrix products, arithmetic and copies ran while one was open for 20% of the time, Pallas kernels for 0%

commit v1 on v0

v1 whole, which is shorter than its diff:
```python
import functools

import jax
import jax.numpy as jnp
from jax import lax
from jax.experimental import pallas as pl
from jax.experimental.pallas import tpu as pltpu
from jax.sharding import PartitionSpec as P

ITERS = 10
W = ITERS
LEV = 6
ROWS, COLS = 24, 512
NT = COLS // 128
RING = NT + 1
FIELDS = 4 * LEV + 1
KX, KY, AREA = 2 * LEV, 3 * LEV, 4 * LEV
PACKS = 3
M0 = 16
M1 = M0 + ROWS
HEIGHT = 56
SHARE = 3
MESH = pl.DeviceIdType.MESH
F32 = jnp.float32


def lanes_of(shape):
    return lax.broadcasted_iota(jnp.int32, shape, len(shape) - 1)


def east(tiles):
    lane = lanes_of(tiles[0].shape)
    turned = [pltpu.roll(t, 127, 1) for t in tiles]
    n = len(tiles)
    return [jnp.where(lane == 127, turned[(i + 1) % n], turned[i]) for i in range(n)]


def west(tiles):
    lane = lanes_of(tiles[0].shape)
    turned = [pltpu.roll(t, 1, 1) for t in tiles]
    n = len(tiles)
    return [jnp.where(lane == 0, turned[(i - 1) % n], turned[i]) for i in range(n)]


def slot(field):
    return field // 12, 10 * (field % 12)


def kernel(
    n_lat, n_lon,
    inc, gain, cx, cy, oc, ar, partner, out,
    inc_v, gain_v, cx_v, cy_v, oc_v, ar_v, part_s,
    D, H1, H2, EX, EY, O, P_, Q, F1, GG, F2,
    in_sem, out_sem, lat_s, lat_r, cor_s, cor_r, lon_s, lon_r,
    f1_s, f1_r, a1_s, a1_r, f2_s, f2_r,
):
    la, lo = lax.axis_index("lat"), lax.axis_index("lon")
    is_top, is_bottom = la == n_lat - 1, la == 0
    not_top, not_bottom = la < n_lat - 1, la > 0
    e_dev, w_dev = (la, lax.rem(lo + 1, n_lon)), (la, lax.rem(lo + n_lon - 1, n_lon))
    n_dev, s_dev = (la + 1, lo), (la - 1, lo)

    def mirror_dev(d):
        return lax.rem(lo + d, n_lon)

    bar = pltpu.get_barrier_semaphore()

    def greet(dev):
        pl.semaphore_signal(bar, inc=1, device_id=dev, device_id_type=MESH)

    greet(e_dev)
    greet(w_dev)

    @pl.when(not_top)
    def _():
        greet(n_dev)

    @pl.when(not_bottom)
    def _():
        greet(s_dev)

    @pl.when(is_top)
    def _():
        for d in range(2, n_lon - 1):
            greet((la, mirror_dev(d)))

    loads = [
        pltpu.make_async_copy(src, dst, in_sem.at[i])
        for i, (src, dst) in enumerate(
            [(oc, oc_v), (ar, ar_v), (cx, cx_v), (cy, cy_v), (gain, gain_v), (inc, inc_v),
             (partner.at[pl.ds(0, 1024)], part_s)]
        )
    ]
    for c in loads:
        c.start()
    for c in loads:
        c.wait()

    for ct in range(NT):
        for r in range(0, ROWS, 8):
            D[AREA, ct, pl.ds(M0 + r, 8), :] = ar_v[pl.ds(r, 8), pl.ds(ct * 128, 128)]

    def prepare(l, _):
        for ct in range(NT):
            cols = pl.ds(ct * 128, 128)
            for r in range(0, ROWS, 8):
                rows, own = pl.ds(r, 8), pl.ds(M0 + r, 8)
                m = oc_v[l, rows, cols].astype(F32)
                am = ar_v[rows, cols] * m
                D[KX + l, ct, own, :] = cx_v[l, rows, cols] * m
                D[KY + l, ct, own, :] = cy_v[l, rows, cols] * m
                for t in range(2):
                    D[t * LEV + l, ct, own, :] = am * (gain_v[t, l, rows, cols] * inc_v[t, l, rows, cols])
        return 0

    lax.fori_loop(0, LEV, prepare, 0)

    lane8 = lanes_of((8, 128))

    def pack(i, _):
        r = pl.multiple_of(i * 8, 8)
        for p in range(PACKS):
            to_e = to_w = None
            for f in range(12 * p, min(12 * p + 12, FIELDS)):
                at = slot(f)[1]
                last = pltpu.roll(D[f, NT - 1, pl.ds(M0 + r, 8), :], (W + at) % 128, 1)
                first = D[f, 0, pl.ds(M0 + r, 8), :]
                if at:
                    first = pltpu.roll(first, at, 1)
                to_e = last if to_e is None else jnp.where(lane8 >= at, last, to_e)
                to_w = first if to_w is None else jnp.where(lane8 >= at, first, to_w)
            P_[0, p, pl.ds(r, 8), :] = to_e
            P_[1, p, pl.ds(r, 8), :] = to_w
        return 0

    lax.fori_loop(0, ROWS // 8, pack, 0)

    def remote(src, dst, ss, rs, dev):
        return pltpu.make_async_remote_copy(
            src_ref=src, dst_ref=dst, send_sem=ss, recv_sem=rs, device_id=dev, device_id_type=MESH
        )

    own_q = Q.at[0, :, pl.ds(M0, ROWS), :], Q.at[1, :, pl.ds(M0, ROWS), :]
    lon = [
        remote(P_.at[0], own_q[0], lon_s.at[0], lon_r.at[0], e_dev),
        remote(P_.at[1], own_q[1], lon_s.at[1], lon_r.at[1], w_dev),
    ]
    main = pl.ds(0, NT)
    low, high = pl.ds(M0, W), pl.ds(M1 - W, W)
    below, above = pl.ds(M0 - W, W), pl.ds(M1, W)
    north = remote(D.at[:, main, high, :], D.at[:, main, below, :], lat_s.at[0], lat_r.at[0], n_dev)
    south = remote(D.at[:, main, low, :], D.at[:, main, above, :], lat_s.at[1], lat_r.at[1], s_dev)
    cor_n = remote(Q.at[:, :, high, :], Q.at[:, :, below, :], cor_s.at[0], cor_r.at[0], n_dev)
    cor_s_ = remote(Q.at[:, :, low, :], Q.at[:, :, above, :], cor_s.at[1], cor_r.at[1], s_dev)

    def share1(d):
        peer = mirror_dev(d)
        dev = (la, peer)
        return (
            remote(D.at[pl.ds(SHARE * peer, SHARE), main, high, :],
                   F1.at[lo, pl.ds(0, SHARE), :, pl.ds(0, W), :], f1_s.at[d], f1_r.at[d], dev),
            remote(D.at[pl.ds(AREA, 1), main, high, :],
                   F1.at[lo, pl.ds(SHARE, 1), :, pl.ds(0, W), :], a1_s.at[d], a1_r.at[d], dev),
        )

    def share2(d):
        peer = mirror_dev(d)
        return remote(F2.at[peer, :, :, pl.ds(0, W), :],
                      D.at[pl.ds(SHARE * lo, SHARE), :, above, :], f2_s.at[d], f2_r.at[d], (la, peer))

    pl.semaphore_wait(bar, jnp.where(is_top, n_lon, jnp.where(is_bottom, 3, 4)))

    for c in lon:
        c.start()

    @pl.when(is_top)
    def _():
        for d in range(1, n_lon):
            for c in share1(d):
                c.start()

    @pl.when(not_top)
    def _():
        north.start()

    @pl.when(not_bottom)
    def _():
        south.start()

    @pl.when(is_top)
    def _():
        keep = [
            pltpu.make_async_copy(D.at[pl.ds(SHARE * lo, SHARE), main, high, :],
                                  F1.at[lo, pl.ds(0, SHARE), :, pl.ds(0, W), :], f1_s.at[0]),
            pltpu.make_async_copy(D.at[pl.ds(AREA, 1), main, high, :],
                                  F1.at[lo, pl.ds(SHARE, 1), :, pl.ds(0, W), :], a1_s.at[0]),
        ]
        for c in keep:
            c.start()
        for c in keep:
            c.wait()

    @pl.when(is_bottom)
    def _():
        def clear(f, _):
            for ct in range(RING):
                for r in (M0 - W, M0 - 8):
                    D[f, ct, pl.ds(r, 8), :] = jnp.zeros((8, 128), F32)
            return 0

        lax.fori_loop(0, FIELDS, clear, 0)

    def unpack(r):
        for p in range(PACKS):
            w_side, e_side = Q[0, p, pl.ds(r, 8), :], Q[1, p, pl.ds(r, 8), :]
            for f in range(12 * p, min(12 * p + 12, FIELDS)):
                at = slot(f)[1]
                wv = pltpu.roll(w_side, (128 - W - at) % 128, 1)
                ev = pltpu.roll(e_side, (128 - at) % 128, 1) if at else e_side
                D[f, NT, pl.ds(r, 8), :] = jnp.where(lane8 < 64, ev, wv)

    for c in lon:
        c.wait_recv()

    @pl.when(not_top)
    def _():
        cor_n.start()

    @pl.when(not_bottom)
    def _():
        cor_s_.start()

    def unpack_own(i, _):
        unpack(M0 + pl.multiple_of(i * 8, 8))
        return 0

    lax.fori_loop(0, ROWS // 8, unpack_own, 0)

    @pl.when(is_top)
    def _():
        for d in range(1, n_lon):
            for c in share1(d):
                c.wait_recv()
        pivot = part_s[0]
        cq, cr = pivot // 128, lax.rem(pivot, 128)
        lane_from = (cr - lane8) & 127
        row_from = 7 - lax.broadcasted_iota(jnp.int32, (8, 128), 0)

        def flip(x):
            return jnp.take_along_axis(jnp.take_along_axis(x, row_from, axis=0), lane_from, axis=1)

        def turn(s, _):
            for ct in range(NT):
                for f in range(SHARE + 1):
                    GG[s * NT + ct, f, pl.ds(0, 8), :] = flip(F1[s, f, ct, pl.ds(2, 8), :])
                    GG[s * NT + ct, f, pl.ds(2, 8), :] = flip(F1[s, f, ct, pl.ds(0, 8), :])
            return 0

        lax.fori_loop(0, n_lon, turn, 0)
        lane16 = lanes_of((16, 128))
        tiles = n_lon * NT

        def image(m, ct, f):
            at = (cq - NT * m - ct + 2 * tiles) % tiles
            return jnp.where(lane16 <= cr, GG[at, f], GG[(at + tiles - 1) % tiles, f])

        def ring_image(m, ct, f):
            if ct < NT:
                return image(m, ct, f)
            return jnp.where(lane16 < 64, image(m, NT, f), image(m, -1, f))

        def send_image(m, _):
            for f in range(SHARE):
                for ct in range(RING):
                    F2[m, f, ct] = ring_image(m, ct, f)
            return 0

        lax.fori_loop(0, n_lon, send_image, 0)
        for d in range(1, n_lon):
            share2(d).start()
        keep = pltpu.make_async_copy(F2.at[lo, :, :, pl.ds(0, W), :],
                                     D.at[pl.ds(SHARE * lo, SHARE), :, above, :], f2_s.at[0])
        keep.start()
        for ct in range(RING):
            D[AREA, ct, above, :] = ring_image(lo, ct, SHARE)[:W]
        keep.wait()

    @pl.when(not_bottom)
    def _():
        cor_n.wait_recv()
        for r in (M0 - W, M0 - 8):
            unpack(r)
        north.wait_recv()

    @pl.when(not_top)
    def _():
        cor_s_.wait_recv()
        for r in (M1, M1 + W - 8):
            unpack(r)
        south.wait_recv()

    @pl.when(is_top)
    def _():
        for d in range(1, n_lon):
            share2(d).wait_recv()

    def wet(x):
        return jnp.where(x != 0.0, 1.0, 0.0).astype(F32)

    def faces(l, _):
        for r in range(M0 - W, M1 + W, 8):
            rows, upper = pl.ds(r, 8), pl.ds(r + 1, 8)
            kx = [D[KX + l, ct, rows, :] for ct in range(RING)]
            for ct, me in enumerate(east([wet(x) for x in kx])):
                EX[l, ct, rows, :] = kx[ct] * me
                EY[l, ct, rows, :] = D[KY + l, ct, rows, :] * wet(D[KX + l, ct, upper, :])
        return 0

    lax.fori_loop(0, LEV, faces, 0)

    @pl.when(is_top)
    def _():
        def fold_faces(l, _):
            for r in (M1, M1 + W - 8):
                rows, upper = pl.ds(r, 8), pl.ds(r + 1, 8)
                kx = [D[KX + l, ct, rows, :] for ct in range(RING)]
                for ct, xe in enumerate(east(kx)):
                    m = wet(kx[ct])
                    EX[l, ct, rows, :] = xe * m
                    EY[l, ct, rows, :] = D[KY + l, ct, upper, :] * m
            here, there = pl.ds(M1 - 1, 1), pl.ds(M1, 1)
            for ct in range(RING):
                EY[l, ct, here, :] = 0.5 * (
                    D[KY + l, ct, here, :] * wet(D[KX + l, ct, there, :])
                    + D[KY + l, ct, there, :] * wet(D[KX + l, ct, here, :])
                )
            return 0

        lax.fori_loop(0, LEV, fold_faces, 0)

    def steps(k, src, dst):
        lower = M0 - W + k
        count = -(-(ROWS + 2 * (W - k)) // 8)

        def level(l, _):
            for i in range(count):
                r = lower + 8 * i
                rows, up, down = pl.ds(r, 8), pl.ds(r + 1, 8), pl.ds(r - 1, 8)
                ex = [EX[l, ct, rows, :] for ct in range(RING)]
                for t in range(2):
                    f = t * LEV + l
                    h = [src[f, ct, rows, :] for ct in range(RING)]
                    fx = [e * (he - hc) for e, he, hc in zip(ex, east(h), h)]
                    fw = west(fx)
                    for ct in range(RING if k < W else NT):
                        d = (fx[ct] - fw[ct]) + (
                            EY[l, ct, rows, :] * (src[f, ct, up, :] - h[ct])
                            - EY[l, ct, down, :] * (h[ct] - src[f, ct, down, :])
                        )
                        a = D[AREA, ct, rows, :]
                        if k < W:
                            dst[f, ct, rows, :] = h[ct] + a * d
                        else:
                            O[t, l, pl.ds(r - M0, 8), pl.ds(ct * 128, 128)] = h[ct] / a + d
            if k == W:
                for t in range(2):
                    pltpu.make_async_copy(O.at[t, l], out.at[t, l], out_sem.at[t, l]).start()
            return 0

        lax.fori_loop(0, LEV, level, 0)

    src, spare = D, (H1, H2)
    for k in range(1, W + 1):
        dst = spare[k % 2]
        steps(k, src, dst)
        src = dst

    for c in lon:
        c.wait_send()

    @pl.when(not_top)
    def _():
        north.wait_send()
        cor_n.wait_send()

    @pl.when(not_bottom)
    def _():
        south.wait_send()
        cor_s_.wait_send()

    @pl.when(is_top)
    def _():
        for d in range(1, n_lon):
            for c in share1(d):
                c.wait_send()
            share2(d).wait_send()

    for t in range(2):
        for l in range(LEV):
            pltpu.make_async_copy(O.at[t, l], out.at[t, l], out_sem.at[t, l]).wait()


def on_device(n_lat, n_lon, *args):
    vmem = lambda *shape: pltpu.VMEM(shape, F32)
    dma = lambda *shape: pltpu.SemaphoreType.DMA(shape)
    scratch = [
        vmem(2, LEV, ROWS, COLS), vmem(2, LEV, ROWS, COLS), vmem(LEV, ROWS, COLS), vmem(LEV, ROWS, COLS),
        pltpu.VMEM((LEV, ROWS, COLS), jnp.int32), vmem(ROWS, COLS), pltpu.SMEM((1024,), jnp.int32),
        vmem(FIELDS, RING, HEIGHT, 128), vmem(2 * LEV, RING, HEIGHT, 128), vmem(2 * LEV, RING, HEIGHT, 128),
        vmem(LEV, RING, HEIGHT, 128), vmem(LEV, RING, HEIGHT, 128), vmem(2, LEV, ROWS, COLS),
        vmem(2, PACKS, ROWS, 128), vmem(2, PACKS, HEIGHT, 128),
        vmem(n_lon, SHARE + 1, NT, 16, 128), vmem(n_lon * NT, SHARE + 1, 16, 128),
        vmem(n_lon, SHARE, RING, 16, 128),
        dma(7), dma(2, LEV), dma(2), dma(2), dma(2), dma(2), dma(2), dma(2),
        dma(n_lon), dma(n_lon), dma(n_lon), dma(n_lon), dma(n_lon), dma(n_lon),
    ]
    return pl.pallas_call(
        functools.partial(kernel, n_lat, n_lon),
        out_shape=jax.ShapeDtypeStruct((2, LEV, ROWS, COLS), F32),
        in_specs=[pl.BlockSpec(memory_space=pl.ANY)] * 7,
        out_specs=pl.BlockSpec(memory_space=pl.ANY),
        scratch_shapes=scratch,
        compiler_params=pltpu.CompilerParams(
            collective_id=0, has_side_effects=True, vmem_limit_bytes=40 * 2**20
        ),
    )(*args)


def solution(mesh):
    in_specs = (
        P(None, None, "lat", "lon"),
        P(None, None, "lat", "lon"),
        P(None, "lat", "lon"),
        P(None, "lat", "lon"),
        P(None, "lat", "lon"),
        P("lat", "lon"),
        P(),
    )
    out_specs = P(None, None, "lat", "lon")
    return jax.shard_map(
        functools.partial(on_device, mesh.shape["lat"], mesh.shape["lon"]),
        mesh=mesh, in_specs=in_specs, out_specs=out_specs, check_vma=False,
    )
```

time: 789 us -> 49.7 us (0.06); the launches traced: 775 us -> 49.3 us
  blocking collectives: 327 us -> 0 us
  local copies, waits for them, and re-layouts: 161 us -> 7.34 us
  starting transfers between devices: 142 us -> 0 us
  other arithmetic: 101 us -> 0 us
  waiting for transfers between devices: 42.5 us -> 0 us
  Pallas kernels: 0 us -> 41.9 us
    all_gather x11 -> x0, blocking collectives: 327 us -> none  [the longest x10 281 us: on_device(): whole_row = lax.all_gather(own_row, 'lon', axis=2, tiled=True)]
    ppermute x44 -> x0, starting transfers between devices: 142 us -> none  [the longest x22 114 us: padded(): lax.ppermute(head, axis, [((i + 1) % count, i) for i in range(count)])]
    gather x16 -> x0, local copies, waits for them, and re-layouts: 56 us -> none  [the longest x10 36.8 us: on_device(): partner_scaled = area_mirror * jnp.take(whole_row, mirror_now, axis=2)]
    all_gather x10 -> x0, local copies, waits for them, and re-layouts: 43.7 us -> none  [on_device(): whole_row = lax.all_gather(own_row, 'lon', axis=2, tiled=True)]
    ppermute x44 -> x0, waiting for transfers between devices: 42.5 us -> none  [the longest x22 23.8 us: padded(): lax.ppermute(head, axis, [((i + 1) % count, i) for i in range(count)])]
    pallas_call x0 -> x1, Pallas kernels: none -> 41.9 us  [on_device(): pl.pallas_call(functools.partial(kernel, n_lat, n_lon), out_shape=jax.Sha...]
    mul x22 -> x0, other arithmetic: 35 us -> none  [the longest x10 31.6 us: on_device(): ef_now[:, 1:-1] * (partner_scaled[:, :, 1:-1] - scaled[:, :, top_row, 1:-1])]
    select_n x19 -> x0, other arithmetic: 24.3 us -> none  [the longest x11 23.7 us: on_device(): partner_scaled = area_mirror * jnp.take(whole_row, mirror_now, axis=2)]
  transfers between devices with their start and end apart: 44 -> 0, of which waited for: 21 -> 0; matrix products, arithmetic and copies ran while one was open for 20% -> 0% of each run, Pallas kernels for 0% -> 0%
where the time goes in v1:
time: 49.7 us; the launch traced here: 49.3 us
  Pallas kernels  41.9 us (84%)
  local copies, waits for them, and re-layouts  7.34 us (15%)
    pallas_call x1, Pallas kernels, on_device(): pl.pallas_call(functools.partial(kernel, n_lat, n_lon), out_shape=jax.Sha...  41.9 us
    unnamed x15, local copies, waits for them, and re-layouts  7.34 us

profile of v1, /device:TPU:225, one launch (start us, length us, event | category | flops | bytes accessed | tf_op | source)
XLA Modules:
  0.0 49.3 jit_solution(17769000559251080337)
XLA Ops:
  0.0 0.0 copy-start
  0.0 1.1 %copy-done = f32[2,6,24,512]{3,2,1,0:T(8,128)S(1)} copy-done((f32[2,6,24,512]{3,2,1,0:T(8,128)S(1)}, f32[2,6,24,512]{3,2,1,0:T(8,128)}, u32[]{:S(2)}) %copy-start) | copy-done | bytes 589848
  1.1 0.0 copy-start.1
  1.1 1.1 %copy-done.1 = f32[2,6,24,512]{3,2,1,0:T(8,128)S(1)} copy-done((f32[2,6,24,512]{3,2,1,0:T(8,128)S(1)}, f32[2,6,24,512]{3,2,1,0:T(8,128)}, u32[]{:S(2)}) %copy-start.1) | copy-done | bytes 589848
  2.1 0.0 copy-start.2
  2.1 1.0 %copy-done.2 = f32[6,24,512]{2,1,0:T(8,128)S(1)} copy-done((f32[6,24,512]{2,1,0:T(8,128)S(1)}, f32[6,24,512]{2,1,0:T(8,128)}, u32[]{:S(2)}) %copy-start.2) | copy-done | bytes 294936
  3.1 0.0 copy-start.3
  3.1 1.0 %copy-done.3 = f32[6,24,512]{2,1,0:T(8,128)S(1)} copy-done((f32[6,24,512]{2,1,0:T(8,128)S(1)}, f32[6,24,512]{2,1,0:T(8,128)}, u32[]{:S(2)}) %copy-start.3) | copy-done | bytes 294936
  4.1 0.0 copy-start.4
  4.1 1.0 %copy-done.4 = s32[6,24,512]{2,1,0:T(8,128)S(1)} copy-done((s32[6,24,512]{2,1,0:T(8,128)S(1)}, s32[6,24,512]{2,1,0:T(8,128)}, u32[]{:S(2)}) %copy-start.4) | copy-done | bytes 294936
  5.0 0.0 copy-start.5
  5.0 0.8 %copy-done.5 = f32[24,512]{1,0:T(8,128)S(1)} copy-done((f32[24,512]{1,0:T(8,128)S(1)}, f32[24,512]{1,0:T(8,128)}, u32[]{:S(2)}) %copy-start.5) | copy-done | bytes 49176
  5.8 0.0 copy-start.6
  5.8 0.7 %copy-done.6 = s32[4096]{0:T(1024)S(1)} copy-done((s32[4096]{0:T(1024)S(1)}, s32[4096]{0:T(1024)}, u32[]{:S(2)}) %copy-start.6) | copy-done | bytes 16408
  6.5 41.9 %shard_map.73 = f32[2,6,24,512]{3,2,1,0:T(8,128)S(1)} custom-call(f32[2,6,24,512]{3,2,1,0:T(8,128)S(1)} %copy-done, f32[2,6,24,512]{3,2,1,0:T(8,128)S(1)} %copy-done.1, f32[6,24,512]{2,1,0:T(8,128)S(1)} %copy-done.2, f32[6,24,512]{2,1,0:T(8,128)S(1)} %copy-done.3, s32[6,24,512]{2,1,0:T(8,128)S(1)} %copy-done.4, f32[24,512]{1,0:T(8,128)S(1)} %copy-done.5, ...), custom_call_target="tpu_custom_call" | custom-call | tf_op jit(solution)/shard_map/pallas_call | solution.py:417
  48.5 0.8 %copy.9 = f32[2,6,24,512]{3,2,1,0:T(8,128)} copy(f32[2,6,24,512]{3,2,1,0:T(8,128)S(1)} %shard_map.73) | data formatting | bytes 1179648
Async XLA Ops:
  0.0 1.1 %copy-start = (f32[2,6,24,512]{3,2,1,0:T(8,128)S(1)}, f32[2,6,24,512]{3,2,1,0:T(8,128)}, u32[]{:S(2)}) copy-start(f32[2,6,24,512]{3,2,1,0:T(8,128)} %inc.1) | copy-start | bytes 1769476
  1.1 1.1 %copy-start.1 = (f32[2,6,24,512]{3,2,1,0:T(8,128)S(1)}, f32[2,6,24,512]{3,2,1,0:T(8,128)}, u32[]{:S(2)}) copy-start(f32[2,6,24,512]{3,2,1,0:T(8,128)} %gain.1) | copy-start | bytes 1769476
  2.1 1.0 %copy-start.2 = (f32[6,24,512]{2,1,0:T(8,128)S(1)}, f32[6,24,512]{2,1,0:T(8,128)}, u32[]{:S(2)}) copy-start(f32[6,24,512]{2,1,0:T(8,128)} %cx.1) | copy-start | bytes 884740
  3.1 1.0 %copy-start.3 = (f32[6,24,512]{2,1,0:T(8,128)S(1)}, f32[6,24,512]{2,1,0:T(8,128)}, u32[]{:S(2)}) copy-start(f32[6,24,512]{2,1,0:T(8,128)} %cy.1) | copy-start | bytes 884740
  4.1 1.0 %copy-start.4 = (s32[6,24,512]{2,1,0:T(8,128)S(1)}, s32[6,24,512]{2,1,0:T(8,128)}, u32[]{:S(2)}) copy-start(s32[6,24,512]{2,1,0:T(8,128)} %oc.1) | copy-start | bytes 884740
  5.0 0.8 %copy-start.5 = (f32[24,512]{1,0:T(8,128)S(1)}, f32[24,512]{1,0:T(8,128)}, u32[]{:S(2)}) copy-start(f32[24,512]{1,0:T(8,128)} %ar.1) | copy-start | bytes 147460
  5.8 0.7 %copy-start.6 = (s32[4096]{0:T(1024)S(1)}, s32[4096]{0:T(1024)}, u32[]{:S(2)}) copy-start(s32[4096]{0:T(1024)} %partner.1) | copy-start | bytes 49156

commit v2 on v1

v2 whole, which is shorter than its diff:
```python
import functools
import itertools

import jax
import jax.numpy as jnp
from jax import lax
from jax.experimental import pallas as pl
from jax.experimental.pallas import tpu as pltpu
from jax.sharding import PartitionSpec as P

ITERS = 10
W = ITERS
LEV = 6
ROWS, COLS = 24, 512
NT = COLS // 128
RING = NT + 1
FIELDS = 4 * LEV + 1
KX, KY, AREA = 2 * LEV, 3 * LEV, 4 * LEV
PACKS = 3
M0 = 16
M1 = M0 + ROWS
HEIGHT = 56
GROUP = 128 // NT
LEVELS_AT_ONCE = 3
SHARE = 3
MESH = pl.DeviceIdType.MESH
F32 = jnp.float32


def lanes_of(shape):
    return lax.broadcasted_iota(jnp.int32, shape, len(shape) - 1)


def pick(choices, by):
    out = choices[-1]
    for i in range(len(choices) - 2, -1, -1):
        out = jnp.where(by == i, choices[i], out)
    return out


def take(x, lanes):
    return jnp.take_along_axis(x, lanes, axis=1)


def interleave(tiles):
    lane = lanes_of(tiles[0].shape)
    group, place = lane // GROUP, lane % GROUP
    sorted_ = [take(x, NT * place + (group - j + NT) % NT) for j, x in enumerate(tiles)]
    mixed = [pick([sorted_[(g - c) % NT] for g in range(NT)], group) for c in range(NT)]
    return [pltpu.roll(x, (128 - GROUP * c) % 128, 1) if c else x for c, x in enumerate(mixed)]


def in_order(tiles):
    lane = lanes_of(tiles[0].shape)
    group = lane // GROUP
    mixed = [pltpu.roll(x, GROUP * c, 1) if c else x for c, x in enumerate(tiles)]
    sorted_ = [pick([mixed[(g - j) % NT] for g in range(NT)], group) for j in range(NT)]
    return [take(x, GROUP * ((lane % NT + j) % NT) + lane // NT) for j, x in enumerate(sorted_)]


def east(x):
    last = lanes_of(x[0].shape) == 127
    main, halo = pltpu.roll(x[0], 127, 1), pltpu.roll(x[NT], 127, 1)
    return x[1:NT] + [jnp.where(last, halo, main), jnp.where(last, main, halo)]


def west(x):
    first = lanes_of(x[0].shape) == 0
    main, halo = pltpu.roll(x[NT - 1], 1, 1), pltpu.roll(x[NT], 1, 1)
    return [jnp.where(first, halo, main)] + x[: NT - 1] + [jnp.where(first, main, halo)]


def slot(field):
    return field // 12, 10 * (field % 12)


def wet(masked):
    return jnp.where(masked != 0.0, 1.0, 0.0).astype(F32)


def inner_rows(k):
    n = ROWS - 2 * k
    if n < 8:
        return [M0 + ROWS // 2 - 4]
    chunks = [M0 + k + 8 * j for j in range(n // 8)]
    return chunks + [M1 - k - 8] if n % 8 else chunks


def kernel(
    n_lat, n_lon,
    inc, gain, cx, cy, oc, ar, partner, out,
    inc_v, gain_v, cx_v, cy_v, oc_v, ar_v, part_s,
    D, H1, H2, H3, H4, H5, H6, H7, H8, H9, C0, CE, CW, CN, CS, RA, O, EDGE, P_, Q, F1, GG, F2,
    in_sem, out_sem, lat_s, lat_r, cor_s, cor_r, lon_s, lon_r, f1_s, f1_r, f2_s, f2_r,
):
    la, lo = lax.axis_index("lat"), lax.axis_index("lon")
    is_top, is_bottom = la == n_lat - 1, la == 0
    not_top, not_bottom = la < n_lat - 1, la > 0
    e_dev, w_dev = (la, lax.rem(lo + 1, n_lon)), (la, lax.rem(lo + n_lon - 1, n_lon))
    n_dev, s_dev = (la + 1, lo), (la - 1, lo)

    def mirror_dev(d):
        return lax.rem(lo + d, n_lon)

    bar = pltpu.get_barrier_semaphore()

    def greet(dev):
        pl.semaphore_signal(bar, inc=1, device_id=dev, device_id_type=MESH)

    greet(e_dev)
    greet(w_dev)

    @pl.when(not_top)
    def _():
        greet(n_dev)

    @pl.when(not_bottom)
    def _():
        greet(s_dev)

    @pl.when(is_top)
    def _():
        for d in range(2, n_lon - 1):
            greet((la, mirror_dev(d)))

    loads = [
        pltpu.make_async_copy(src, dst, in_sem.at[i])
        for i, (src, dst) in enumerate(
            [(oc, oc_v), (ar, ar_v), (cx, cx_v), (cy, cy_v), (gain, gain_v), (inc, inc_v),
             (partner.at[pl.ds(0, 1024)], part_s)]
        )
    ]
    for c in loads:
        c.start()
    def place(field, r, tiles):
        EDGE[field, 0, pl.ds(r, 8), :] = tiles[0]
        EDGE[field, 1, pl.ds(r, 8), :] = tiles[NT - 1]
        for c, x in enumerate(interleave(tiles)):
            D[field, c, pl.ds(M0 + r, 8), :] = x

    runs = [pl.ds(j * 128, 128) for j in range(NT)]

    def faces(i, _):
        for l in (2 * i, 2 * i + 1):
            for r in range(0, ROWS, 8):
                rows = pl.ds(r, 8)
                m = [oc_v[l, rows, j].astype(F32) for j in runs]
                place(KX + l, r, [cx_v[l, rows, j] * mj for j, mj in zip(runs, m)])
                place(KY + l, r, [cy_v[l, rows, j] * mj for j, mj in zip(runs, m)])
        return 0

    def cells(i, _):
        for l in (2 * i, 2 * i + 1):
            for r in range(0, ROWS, 8):
                rows = pl.ds(r, 8)
                am = [ar_v[rows, j] * oc_v[l, rows, j].astype(F32) for j in runs]
                for t in range(2):
                    place(t * LEV + l, r,
                          [x * (gain_v[t, l, rows, j] * inc_v[t, l, rows, j]) for j, x in zip(runs, am)])
        return 0

    for c in loads[:4]:
        c.wait()
    for r in range(0, ROWS, 8):
        place(AREA, r, [ar_v[pl.ds(r, 8), j] for j in runs])
    lax.fori_loop(0, LEV // 2, faces, 0)
    for c in loads[4:]:
        c.wait()
    lax.fori_loop(0, LEV // 2, cells, 0)

    lane8 = lanes_of((8, 128))

    def pack(i, _):
        rows = pl.ds(pl.multiple_of(i * 8, 8), 8)
        for p in range(PACKS):
            to_e = to_w = None
            for f in range(12 * p, min(12 * p + 12, FIELDS)):
                at = slot(f)[1]
                last = pltpu.roll(EDGE[f, 1, rows, :], (W + at) % 128, 1)
                first = EDGE[f, 0, rows, :]
                if at:
                    first = pltpu.roll(first, at, 1)
                to_e = last if to_e is None else jnp.where(lane8 >= at, last, to_e)
                to_w = first if to_w is None else jnp.where(lane8 >= at, first, to_w)
            P_[0, p, rows, :] = to_e
            P_[1, p, rows, :] = to_w
        return 0


    def remote(src, dst, ss, rs, dev):
        return pltpu.make_async_remote_copy(
            src_ref=src, dst_ref=dst, send_sem=ss, recv_sem=rs, device_id=dev, device_id_type=MESH
        )

    own_q = Q.at[0, :, pl.ds(M0, ROWS), :], Q.at[1, :, pl.ds(M0, ROWS), :]
    lon = [
        remote(P_.at[0], own_q[0], lon_s.at[0], lon_r.at[0], e_dev),
        remote(P_.at[1], own_q[1], lon_s.at[1], lon_r.at[1], w_dev),
    ]
    main = pl.ds(0, NT)
    low, high = pl.ds(M0, W), pl.ds(M1 - W, W)
    below, above = pl.ds(M0 - W, W), pl.ds(M1, W)
    north = remote(D.at[:, main, high, :], D.at[:, main, below, :], lat_s.at[0], lat_r.at[0], n_dev)
    south = remote(D.at[:, main, low, :], D.at[:, main, above, :], lat_s.at[1], lat_r.at[1], s_dev)
    cor_n = remote(Q.at[:, :, high, :], Q.at[:, :, below, :], cor_s.at[0], cor_r.at[0], n_dev)
    cor_s_ = remote(Q.at[:, :, low, :], Q.at[:, :, above, :], cor_s.at[1], cor_r.at[1], s_dev)

    def share1(f, d):
        peer = mirror_dev(d)
        field = AREA if f == SHARE else SHARE * peer + f
        return remote(D.at[pl.ds(field, 1), main, high, :], F1.at[lo, pl.ds(f, 1), :, pl.ds(0, W), :],
                      f1_s.at[f, d], f1_r.at[f, d], (la, peer))

    def share2(f, d):
        peer = mirror_dev(d)
        return remote(F2.at[peer, pl.ds(f, 1), :, pl.ds(0, W), :], D.at[pl.ds(SHARE * lo + f, 1), :, above, :],
                      f2_s.at[f, d], f2_r.at[f, d], (la, peer))

    lax.fori_loop(0, ROWS // 8, pack, 0)

    pl.semaphore_wait(bar, jnp.where(is_top, n_lon, jnp.where(is_bottom, 3, 4)))

    for c in lon:
        c.start()

    @pl.when(is_top)
    def _():
        for f in range(SHARE + 1):
            for d in range(1, n_lon):
                share1(f, d).start()

    @pl.when(not_top)
    def _():
        north.start()

    @pl.when(not_bottom)
    def _():
        south.start()

    @pl.when(is_top)
    def _():
        keep = [
            pltpu.make_async_copy(D.at[pl.ds(SHARE * lo, SHARE), main, high, :],
                                  F1.at[lo, pl.ds(0, SHARE), :, pl.ds(0, W), :], f1_s.at[0, 0]),
            pltpu.make_async_copy(D.at[pl.ds(AREA, 1), main, high, :],
                                  F1.at[lo, pl.ds(SHARE, 1), :, pl.ds(0, W), :], f1_s.at[1, 0]),
        ]
        for c in keep:
            c.start()
        for c in keep:
            c.wait()

    @pl.when(is_bottom)
    def _():
        def clear(f, _):
            for ct in range(RING):
                for r in (M0 - W, M0 - 8):
                    D[f, ct, pl.ds(r, 8), :] = jnp.zeros((8, 128), F32)
            return 0

        lax.fori_loop(0, FIELDS, clear, 0)

    for c in range(NT):
        for r in range(M0, M1, 8):
            RA[c, pl.ds(r, 8), :] = 1.0 / D[AREA, c, pl.ds(r, 8), :]

    def unpack(r):
        for p in range(PACKS):
            w_side, e_side = Q[0, p, pl.ds(r, 8), :], Q[1, p, pl.ds(r, 8), :]
            for f in range(12 * p, min(12 * p + 12, FIELDS)):
                at = slot(f)[1]
                wv = pltpu.roll(w_side, (128 - W - at) % 128, 1)
                ev = pltpu.roll(e_side, (128 - at) % 128, 1) if at else e_side
                D[f, NT, pl.ds(r, 8), :] = jnp.where(lane8 < 64, ev, wv)

    def weights(chunks, fold):
        def levels(i, _):
            for l, r in itertools.product([LEVELS_AT_ONCE * i + q for q in range(LEVELS_AT_ONCE)], chunks):
                rows, up, down = pl.ds(r, 8), pl.ds(r + 1, 8), pl.ds(r - 1, 8)
                row = r + lax.broadcasted_iota(jnp.int32, (8, 128), 0)
                kx = [D[KX + l, ct, rows, :] for ct in range(RING)]
                m = [wet(x) for x in kx]
                ex = [k * n for k, n in zip(kx, east(m))]
                if fold:
                    ex = [jnp.where(row >= M1, k * n, x) for k, n, x in zip(east(kx), m, ex)]
                for ct, ew in enumerate(west(ex)):
                    ky, ky_s = D[KY + l, ct, rows, :], D[KY + l, ct, down, :]
                    m_n = wet(D[KX + l, ct, up, :])
                    yn, ys = ky * m_n, ky_s * m[ct]
                    if fold:
                        ky_n, m_s = D[KY + l, ct, up, :], wet(D[KX + l, ct, down, :])
                        yn_f, ys_f = ky_n * m[ct], ky * m_s
                        yn = jnp.where(row >= M1, yn_f, jnp.where(row == M1 - 1, 0.5 * (yn + yn_f), yn))
                        ys = jnp.where(row > M1, ys_f, jnp.where(row == M1, 0.5 * (ys + ys_f), ys))
                    a = D[AREA, ct, rows, :]
                    ce, cw, cn, cs = a * ex[ct], a * ew, a * yn, a * ys
                    CE[l, ct, rows, :], CW[l, ct, rows, :] = ce, cw
                    CN[l, ct, rows, :], CS[l, ct, rows, :] = cn, cs
                    C0[l, ct, rows, :] = 1.0 - ((ce + cw) + (cn + cs))
            return 0

        lax.fori_loop(0, LEV // LEVELS_AT_ONCE, levels, 0)

    H = (D, H1, H2, H3, H4, H5, H6, H7, H8, H9)

    def advance(k, chunks):
        src = H[k - 1]

        def levels(i, _):
            for q in range(LEVELS_AT_ONCE):
                l = LEVELS_AT_ONCE * i + q
                for r in chunks:
                    rows, up, down = pl.ds(r, 8), pl.ds(r + 1, 8), pl.ds(r - 1, 8)
                    cs = [[C[l, ct, rows, :] for C in (C0, CE, CW, CN, CS)] for ct in range(RING)]
                    for t in range(2):
                        f = t * LEV + l
                        h = [src[f, ct, rows, :] for ct in range(RING)]
                        he, hw = east(h), west(h)
                        new = []
                        for ct in range(RING if k < ITERS else NT):
                            c0, ce, cw, cn, c_s = cs[ct]
                            new.append((c0 * h[ct] + ce * he[ct]) + (
                                cw * hw[ct] + (cn * src[f, ct, up, :] + c_s * src[f, ct, down, :])))
                        if k < ITERS:
                            for ct in range(RING):
                                H[k][f, ct, rows, :] = new[ct]
                        else:
                            g = in_order([x * RA[ct, rows, :] for ct, x in enumerate(new)])
                            for j in range(NT):
                                O[t, l, j, pl.ds(r - M0, 8), :] = g[j]
            return 0

        lax.fori_loop(0, LEV // LEVELS_AT_ONCE, levels, 0)

    for c in lon:
        c.wait_recv()

    @pl.when(not_top)
    def _():
        cor_n.start()

    @pl.when(not_bottom)
    def _():
        cor_s_.start()

    def unpack_own(i, _):
        unpack(M0 + pl.multiple_of(i * 8, 8))
        return 0

    lax.fori_loop(0, ROWS // 8, unpack_own, 0)
    weights(inner_rows(1), False)

    @pl.when(is_top)
    def _():
        pivot = part_s[0] + n_lon * COLS
        row_from = 7 - lax.broadcasted_iota(jnp.int32, (8, 128), 0)
        lane16 = lanes_of((16, 128))

        def counterpart(c):
            other = lax.rem(pivot - c, NT)
            at = (pivot - c - other) // NT
            return other, at // 128, lax.rem(at, 128)

        def turn(f):
            for s, c in itertools.product(range(n_lon), range(NT)):
                lanes = (counterpart(c)[2] - lane8) & 127
                for to, start in ((0, 2), (2, 0)):
                    x = jnp.take_along_axis(F1[s, f, c, pl.ds(start, 8), :], row_from, axis=0)
                    GG[f, s, c, pl.ds(to, 8), :] = take(x, lanes)

        def image(m, c, f):
            other, at, lane = counterpart(c)
            block = lax.rem(at - m + 2 * n_lon, n_lon)
            return jnp.where(lane16 <= lane, GG[f, block, other],
                             GG[f, lax.rem(block + n_lon - 1, n_lon), other])

        def halo(eastern, western):
            both = [jnp.where(lane16 < 64, e, w) for e, w in zip(eastern, western)]
            lanes = lane16 // NT + jnp.where(lane16 < 64, 0, 128 - GROUP)
            return pick([take(x, lanes) for x in both], lane16 % NT)

        for f in range(SHARE):
            for d in range(1, n_lon):
                share1(f, d).wait_recv()
            turn(f)

            for m, c in itertools.product(range(n_lon), range(NT)):
                F2[m, f, c] = image(m, c, f)
            for m in range(n_lon):
                e, w = (m + 1) % n_lon, (m - 1) % n_lon
                F2[m, f, NT] = halo([F2[e, f, c] for c in range(NT)], [F2[w, f, c] for c in range(NT)])
            for d in range(1, n_lon):
                share2(f, d).start()
        for d in range(1, n_lon):
            share1(SHARE, d).wait_recv()
        turn(SHARE)
        for c in range(NT):
            D[AREA, c, above, :] = image(lo, c, SHARE)[:W]
        e, w = lax.rem(lo + 1, n_lon), lax.rem(lo + n_lon - 1, n_lon)
        D[AREA, NT, above, :] = halo([image(e, c, SHARE) for c in range(NT)],
                                     [image(w, c, SHARE) for c in range(NT)])[:W]
        keep = pltpu.make_async_copy(F2.at[lo, :, :, pl.ds(0, W), :],
                                     D.at[pl.ds(SHARE * lo, SHARE), :, above, :], f2_s.at[0, 0])
        keep.start()
        keep.wait()

    for k in range(1, ITERS + 1):
        advance(k, inner_rows(k))

    def side(i, _):
        northern = i == lax.rem(la, 2)
        southern = i != lax.rem(la, 2)

        @pl.when(southern & not_bottom)
        def _():
            cor_n.wait_recv()
            for r in (M0 - W, M0 - 8):
                unpack(r)
            north.wait_recv()

        @pl.when(southern)
        def _():
            weights((M0 - W + 1, M0 - 7), False)

        @pl.when(northern & not_top)
        def _():
            cor_s_.wait_recv()
            for r in (M1, M1 + W - 8):
                unpack(r)
            south.wait_recv()
            weights((M1 - 1, M1 + W - 9), False)

        @pl.when(northern & is_top)
        def _():
            for f in range(SHARE):
                for d in range(1, n_lon):
                    share2(f, d).wait_recv()
            weights((M1 - 1, M1 + W - 9), True)

        @pl.when(southern)
        def _():
            for k in range(1, ITERS + 1):
                advance(k, (M0 - W + k, M0 - 8 + k))

        @pl.when(northern)
        def _():
            for k in range(1, ITERS + 1):
                advance(k, (M1 - k, M1 + W - 8 - k))

        return 0

    lax.fori_loop(0, 2, side, 0)
    results = [
        pltpu.make_async_copy(O.at[:, :, j], out.at[:, :, :, pl.ds(128 * j, 128)], out_sem.at[j])
        for j in range(NT)
    ]
    for c in results:
        c.start()

    for c in lon:
        c.wait_send()

    @pl.when(not_top)
    def _():
        north.wait_send()
        cor_n.wait_send()

    @pl.when(not_bottom)
    def _():
        south.wait_send()
        cor_s_.wait_send()

    @pl.when(is_top)
    def _():
        for d in range(1, n_lon):
            for f in range(SHARE + 1):
                share1(f, d).wait_send()
            for f in range(SHARE):
                share2(f, d).wait_send()

    for c in results:
        c.wait()


def on_device(n_lat, n_lon, *args):
    vmem = lambda *shape: pltpu.VMEM(shape, F32)
    dma = lambda *shape: pltpu.SemaphoreType.DMA(shape)
    scratch = [
        vmem(2, LEV, ROWS, COLS), vmem(2, LEV, ROWS, COLS), vmem(LEV, ROWS, COLS), vmem(LEV, ROWS, COLS),
        pltpu.VMEM((LEV, ROWS, COLS), jnp.int32), vmem(ROWS, COLS), pltpu.SMEM((1024,), jnp.int32),
        vmem(FIELDS, RING, HEIGHT, 128), *[vmem(2 * LEV, RING, HEIGHT, 128)] * (ITERS - 1),
        *[vmem(LEV, RING, HEIGHT, 128)] * 5, vmem(NT, HEIGHT, 128), vmem(2, LEV, NT, ROWS, 128),
        vmem(FIELDS, 2, ROWS, 128), vmem(2, PACKS, ROWS, 128), vmem(2, PACKS, HEIGHT, 128),
        vmem(n_lon, SHARE + 1, NT, 16, 128), vmem(SHARE + 1, n_lon, NT, 16, 128),
        vmem(n_lon, SHARE, RING, 16, 128),
        dma(7), dma(NT), dma(2), dma(2), dma(2), dma(2), dma(2), dma(2),
        dma(SHARE + 1, n_lon), dma(SHARE + 1, n_lon), dma(SHARE, n_lon), dma(SHARE, n_lon),
    ]
    return pl.pallas_call(
        functools.partial(kernel, n_lat, n_lon),
        out_shape=jax.ShapeDtypeStruct((2, LEV, ROWS, COLS), F32),
        in_specs=[pl.BlockSpec(memory_space=pl.ANY)] * 7,
        out_specs=pl.BlockSpec(memory_space=pl.ANY),
        scratch_shapes=scratch,
        compiler_params=pltpu.CompilerParams(
            collective_id=0, has_side_effects=True, vmem_limit_bytes=60 * 2**20
        ),
    )(*args)


def solution(mesh):
    in_specs = (
        P(None, None, "lat", "lon"),
        P(None, None, "lat", "lon"),
        P(None, "lat", "lon"),
        P(None, "lat", "lon"),
        P(None, "lat", "lon"),
        P("lat", "lon"),
        P(),
    )
    out_specs = P(None, None, "lat", "lon")
    return jax.shard_map(
        functools.partial(on_device, mesh.shape["lat"], mesh.shape["lon"]),
        mesh=mesh, in_specs=in_specs, out_specs=out_specs, check_vma=False,
    )
```

time: 49.7 us -> 34.5 us (0.69)
  Pallas kernels: 41.9 us -> 32.4 us
  local copies, waits for them, and re-layouts: 7.34 us -> 1.92 us
    pallas_call x1, Pallas kernels: 41.9 us -> 32.4 us  [on_device(): pl.pallas_call(functools.partial(kernel, n_lat, n_lon), out_shape=jax.Sha...]
    unnamed x15 -> x1, local copies, waits for them, and re-layouts: 7.34 us -> 1.92 us
where the time goes in v2:
time: 34.5 us; the launch traced here: 34.3 us
  Pallas kernels  32.4 us (94%)
  local copies, waits for them, and re-layouts  1.92 us (6%)
    pallas_call x1, Pallas kernels, on_device(): pl.pallas_call(functools.partial(kernel, n_lat, n_lon), out_shape=jax.Sha...  32.4 us
    unnamed x1, local copies, waits for them, and re-layouts  1.92 us

profile of v2, /device:TPU:225, one launch (start us, length us, event | category | flops | bytes accessed | tf_op | source)
XLA Modules:
  0.0 34.3 jit_solution(11652179689959274710)
XLA Ops:
  0.0 32.4 %shard_map.73 = f32[2,6,24,512]{3,2,1,0:T(8,128)} custom-call(f32[2,6,24,512]{3,2,1,0:T(8,128)} %inc.1, f32[2,6,24,512]{3,2,1,0:T(8,128)} %gain.1, f32[6,24,512]{2,1,0:T(8,128)} %cx.1, f32[6,24,512]{2,1,0:T(8,128)} %cy.1, s32[6,24,512]{2,1,0:T(8,128)} %oc.1, f32[24,512]{1,0:T(8,128)} %ar.1, s32[4096]{0:T(1024)} %partner.1), custom_call_target="tpu_custom_call" | custom-call | tf_op jit(solution)/shard_map/pallas_call | solution.py:499
  32.4 1.9 %copy.9 = f32[2,6,24,512]{3,2,1,0:T(8,128)} copy(f32[2,6,24,512]{3,2,1,0:T(8,128)} %shard_map.73) | data formatting | bytes 1179648

commit v3 on v2

--- a/solution.py
+++ b/solution.py
@@ -132,41 +132,58 @@
     ]
     for c in loads:
         c.start()
+    def edges(field, r, tiles):
+        EDGE[field, 0, pl.ds(r, 8), :] = tiles[0]
+        EDGE[field, 1, pl.ds(r, 8), :] = tiles[-1]
+
     def place(field, r, tiles):
-        EDGE[field, 0, pl.ds(r, 8), :] = tiles[0]
-        EDGE[field, 1, pl.ds(r, 8), :] = tiles[NT - 1]
         for c, x in enumerate(interleave(tiles)):
             D[field, c, pl.ds(M0 + r, 8), :] = x
 
     runs = [pl.ds(j * 128, 128) for j in range(NT)]
 
-    def faces(i, _):
-        for l in (2 * i, 2 * i + 1):
-            for r in range(0, ROWS, 8):
-                rows = pl.ds(r, 8)
-                m = [oc_v[l, rows, j].astype(F32) for j in runs]
-                place(KX + l, r, [cx_v[l, rows, j] * mj for j, mj in zip(runs, m)])
-                place(KY + l, r, [cy_v[l, rows, j] * mj for j, mj in zip(runs, m)])
-        return 0
-
-    def cells(i, _):
-        for l in (2 * i, 2 * i + 1):
-            for r in range(0, ROWS, 8):
-                rows = pl.ds(r, 8)
-                am = [ar_v[rows, j] * oc_v[l, rows, j].astype(F32) for j in runs]
-                for t in range(2):
-                    place(t * LEV + l, r,
-                          [x * (gain_v[t, l, rows, j] * inc_v[t, l, rows, j]) for j, x in zip(runs, am)])
-        return 0
-
+    def faces(put, runs, l):
+        for r in range(0, ROWS, 8):
+            rows = pl.ds(r, 8)
+            m = [oc_v[l, rows, j].astype(F32) for j in runs]
+            put(KX + l, r, [cx_v[l, rows, j] * mj for j, mj in zip(runs, m)])
+            put(KY + l, r, [cy_v[l, rows, j] * mj for j, mj in zip(runs, m)])
+
+    def cells(put, runs, l):
+        for r in range(0, ROWS, 8):
+            rows = pl.ds(r, 8)
+            am = [ar_v[rows, j] * oc_v[l, rows, j].astype(F32) for j in runs]
+            for t in range(2):
+                put(t * LEV + l, r,
+                    [x * (gain_v[t, l, rows, j] * inc_v[t, l, rows, j]) for j, x in zip(runs, am)])
+
+    def area(put, runs):
+        for r in range(0, ROWS, 8):
+            put(AREA, r, [ar_v[pl.ds(r, 8), j] for j in runs])
+
+    def all_levels(what, put, runs):
+        def two(i, _):
+            what(put, runs, 2 * i)
+            what(put, runs, 2 * i + 1)
+            return 0
+
+        lax.fori_loop(0, LEV // 2, two, 0)
+
+    ends = [runs[0], runs[-1]]
     for c in loads[:4]:
         c.wait()
-    for r in range(0, ROWS, 8):
-        place(AREA, r, [ar_v[pl.ds(r, 8), j] for j in runs])
-    lax.fori_loop(0, LEV // 2, faces, 0)
+    area(edges, ends)
+    all_levels(faces, edges, ends)
+    near_top = la >= n_lat - 3
+
+    @pl.when(near_top)
+    def _():
+        area(place, runs)
+        all_levels(faces, place, runs)
+
     for c in loads[4:]:
         c.wait()
-    lax.fori_loop(0, LEV // 2, cells, 0)
+    all_levels(cells, edges, ends)
 
     lane8 = lanes_of((8, 128))
 
@@ -200,20 +217,23 @@
     main = pl.ds(0, NT)
     low, high = pl.ds(M0, W), pl.ds(M1 - W, W)
     below, above = pl.ds(M0 - W, W), pl.ds(M1, W)
-    north = remote(D.at[:, main, high, :], D.at[:, main, below, :], lat_s.at[0], lat_r.at[0], n_dev)
-    south = remote(D.at[:, main, low, :], D.at[:, main, above, :], lat_s.at[1], lat_r.at[1], s_dev)
+    parts = (pl.ds(KX, FIELDS - KX), pl.ds(0, KX))
+    north = [remote(D.at[p, main, high, :], D.at[p, main, below, :], lat_s.at[0, i], lat_r.at[0, i], n_dev)
+             for i, p in enumerate(parts)]
+    south = [remote(D.at[p, main, low, :], D.at[p, main, above, :], lat_s.at[1, i], lat_r.at[1, i], s_dev)
+             for i, p in enumerate(parts)]
     cor_n = remote(Q.at[:, :, high, :], Q.at[:, :, below, :], cor_s.at[0], cor_r.at[0], n_dev)
     cor_s_ = remote(Q.at[:, :, low, :], Q.at[:, :, above, :], cor_s.at[1], cor_r.at[1], s_dev)
 
     def share1(f, d):
         peer = mirror_dev(d)
-        field = AREA if f == SHARE else SHARE * peer + f
+        field = AREA if f == SHARE else n_lon * f + peer
         return remote(D.at[pl.ds(field, 1), main, high, :], F1.at[lo, pl.ds(f, 1), :, pl.ds(0, W), :],
                       f1_s.at[f, d], f1_r.at[f, d], (la, peer))
 
     def share2(f, d):
         peer = mirror_dev(d)
-        return remote(F2.at[peer, pl.ds(f, 1), :, pl.ds(0, W), :], D.at[pl.ds(SHARE * lo + f, 1), :, above, :],
+        return remote(F2.at[peer, pl.ds(f, 1), :, pl.ds(0, W), :], D.at[pl.ds(n_lon * f + lo, 1), :, above, :],
                       f2_s.at[f, d], f2_r.at[f, d], (la, peer))
 
     lax.fori_loop(0, ROWS // 8, pack, 0)
@@ -223,27 +243,40 @@
     for c in lon:
         c.start()
 
+    @pl.when(~near_top)
+    def _():
+        area(place, runs)
+        all_levels(faces, place, runs)
+
     @pl.when(is_top)
     def _():
-        for f in range(SHARE + 1):
+        for d in range(1, n_lon):
+            share1(2, d).start()
+
+    all_levels(cells, place, runs)
+
+    @pl.when(is_top)
+    def _():
+        for f in (1, 0, SHARE):
             for d in range(1, n_lon):
                 share1(f, d).start()
 
-    @pl.when(not_top)
-    def _():
-        north.start()
+    late_n = la == n_lat - 5
+
+    @pl.when(not_top & ~late_n)
+    def _():
+        north[0].start()
 
     @pl.when(not_bottom)
     def _():
-        south.start()
+        south[0].start()
 
     @pl.when(is_top)
     def _():
         keep = [
-            pltpu.make_async_copy(D.at[pl.ds(SHARE * lo, SHARE), main, high, :],
-                                  F1.at[lo, pl.ds(0, SHARE), :, pl.ds(0, W), :], f1_s.at[0, 0]),
-            pltpu.make_async_copy(D.at[pl.ds(AREA, 1), main, high, :],
-                                  F1.at[lo, pl.ds(SHARE, 1), :, pl.ds(0, W), :], f1_s.at[1, 0]),
+            pltpu.make_async_copy(D.at[pl.ds(AREA if f == SHARE else n_lon * f + lo, 1), main, high, :],
+                                  F1.at[lo, pl.ds(f, 1), :, pl.ds(0, W), :], f1_s.at[f, 0])
+            for f in range(SHARE + 1)
         ]
         for c in keep:
             c.start()
@@ -342,6 +375,11 @@
     @pl.when(not_bottom)
     def _():
         cor_s_.start()
+        south[1].start()
+
+    @pl.when(not_top & ~late_n)
+    def _():
+        north[1].start()
 
     def unpack_own(i, _):
         unpack(M0 + pl.multiple_of(i * 8, 8))
@@ -379,11 +417,17 @@
             lanes = lane16 // NT + jnp.where(lane16 < 64, 0, 128 - GROUP)
             return pick([take(x, lanes) for x in both], lane16 % NT)
 
-        for f in range(SHARE):
+        for f in (2, 1, 0, SHARE):
             for d in range(1, n_lon):
                 share1(f, d).wait_recv()
             turn(f)
-
+            if f == SHARE:
+                for c in range(NT):
+                    D[AREA, c, above, :] = image(lo, c, SHARE)[:W]
+                e, w = lax.rem(lo + 1, n_lon), lax.rem(lo + n_lon - 1, n_lon)
+                D[AREA, NT, above, :] = halo([image(e, c, SHARE) for c in range(NT)],
+                                             [image(w, c, SHARE) for c in range(NT)])[:W]
+                continue
             for m, c in itertools.product(range(n_lon), range(NT)):
                 F2[m, f, c] = image(m, c, f)
             for m in range(n_lon):
@@ -391,56 +435,68 @@
                 F2[m, f, NT] = halo([F2[e, f, c] for c in range(NT)], [F2[w, f, c] for c in range(NT)])
             for d in range(1, n_lon):
                 share2(f, d).start()
-        for d in range(1, n_lon):
-            share1(SHARE, d).wait_recv()
-        turn(SHARE)
-        for c in range(NT):
-            D[AREA, c, above, :] = image(lo, c, SHARE)[:W]
-        e, w = lax.rem(lo + 1, n_lon), lax.rem(lo + n_lon - 1, n_lon)
-        D[AREA, NT, above, :] = halo([image(e, c, SHARE) for c in range(NT)],
-                                     [image(w, c, SHARE) for c in range(NT)])[:W]
-        keep = pltpu.make_async_copy(F2.at[lo, :, :, pl.ds(0, W), :],
-                                     D.at[pl.ds(SHARE * lo, SHARE), :, above, :], f2_s.at[0, 0])
-        keep.start()
-        keep.wait()
+        keep = [
+            pltpu.make_async_copy(F2.at[lo, pl.ds(f, 1), :, pl.ds(0, W), :],
+                                  D.at[pl.ds(n_lon * f + lo, 1), :, above, :], f2_s.at[f, 0])
+            for f in range(SHARE)
+        ]
+        for c in keep:
+            c.start()
+        for c in keep:
+            c.wait()
 
     for k in range(1, ITERS + 1):
         advance(k, inner_rows(k))
+
+    @pl.when(late_n)
+    def _():
+        north[0].start()
 
     def side(i, _):
         northern = i == lax.rem(la, 2)
         southern = i != lax.rem(la, 2)
 
+        @pl.when(late_n & (i == 1))
+        def _():
+            north[1].start()
+
         @pl.when(southern & not_bottom)
         def _():
             cor_n.wait_recv()
             for r in (M0 - W, M0 - 8):
                 unpack(r)
-            north.wait_recv()
+            north[0].wait_recv()
 
         @pl.when(southern)
         def _():
             weights((M0 - W + 1, M0 - 7), False)
+
+        @pl.when(southern & not_bottom)
+        def _():
+            north[1].wait_recv()
+
+        @pl.when(southern)
+        def _():
+            for k in range(1, ITERS + 1):
+                advance(k, (M0 - W + k, M0 - 8 + k))
 
         @pl.when(northern & not_top)
         def _():
             cor_s_.wait_recv()
             for r in (M1, M1 + W - 8):
                 unpack(r)
-            south.wait_recv()
+            south[0].wait_recv()
             weights((M1 - 1, M1 + W - 9), False)
+            south[1].wait_recv()
 
         @pl.when(northern & is_top)
         def _():
-            for f in range(SHARE):
+            for f in range(SHARE - 1, 0, -1):
                 for d in range(1, n_lon):
                     share2(f, d).wait_recv()
             weights((M1 - 1, M1 + W - 9), True)
-
-        @pl.when(southern)
-        def _():
-            for k in range(1, ITERS + 1):
-                advance(k, (M0 - W + k, M0 - 8 + k))
+            for d in range(1, n_lon):
+                share2(0, d).wait_recv()
 
         @pl.when(northern)
         def _():
@@ -462,12 +518,14 @@
 
     @pl.when(not_top)
     def _():
-        north.wait_send()
+        for c in north:
+            c.wait_send()
         cor_n.wait_send()
 
     @pl.when(not_bottom)
     def _():
-        south.wait_send()
+        for c in south:
+            c.wait_send()
         cor_s_.wait_send()
 
     @pl.when(is_top)
@@ -493,7 +551,7 @@
         vmem(FIELDS, 2, ROWS, 128), vmem(2, PACKS, ROWS, 128), vmem(2, PACKS, HEIGHT, 128),
         vmem(n_lon, SHARE + 1, NT, 16, 128), vmem(SHARE + 1, n_lon, NT, 16, 128),
         vmem(n_lon, SHARE, RING, 16, 128),
-        dma(7), dma(NT), dma(2), dma(2), dma(2), dma(2), dma(2), dma(2),
+        dma(7), dma(NT), dma(2, 2), dma(2, 2), dma(2), dma(2), dma(2), dma(2),
         dma(SHARE + 1, n_lon), dma(SHARE + 1, n_lon), dma(SHARE, n_lon), dma(SHARE, n_lon),
     ]
     return pl.pallas_call(

time: 34.5 us -> 34 us (0.986)
  Pallas kernels: 32.4 us -> 31.9 us
    pallas_call x1, Pallas kernels: 32.4 us -> 31.9 us  [on_device(): pl.pallas_call(functools.partial(kernel, n_lat, n_lon), out_shape=jax.Sha...]
where the time goes in v3:
time: 34 us; the launch traced here: 33.9 us
  Pallas kernels  31.9 us (94%)
  local copies, waits for them, and re-layouts  1.92 us (6%)
    pallas_call x1, Pallas kernels, on_device(): pl.pallas_call(functools.partial(kernel, n_lat, n_lon), out_shape=jax.Sha...  31.9 us
    unnamed x1, local copies, waits for them, and re-layouts  1.92 us

profile of v3, /device:TPU:225, one launch (start us, length us, event | category | flops | bytes accessed | tf_op | source)
XLA Modules:
  0.0 33.9 jit_solution(13005820184992321889)
XLA Ops:
  0.0 31.9 %shard_map.73 = f32[2,6,24,512]{3,2,1,0:T(8,128)} custom-call(f32[2,6,24,512]{3,2,1,0:T(8,128)} %inc.1, f32[2,6,24,512]{3,2,1,0:T(8,128)} %gain.1, f32[6,24,512]{2,1,0:T(8,128)} %cx.1, f32[6,24,512]{2,1,0:T(8,128)} %cy.1, s32[6,24,512]{2,1,0:T(8,128)} %oc.1, f32[24,512]{1,0:T(8,128)} %ar.1, s32[4096]{0:T(1024)} %partner.1), custom_call_target="tpu_custom_call" | custom-call | tf_op jit(solution)/shard_map/pallas_call | solution.py:557
  31.9 1.9 %copy.9 = f32[2,6,24,512]{3,2,1,0:T(8,128)} copy(f32[2,6,24,512]{3,2,1,0:T(8,128)} %shard_map.73) | data formatting | bytes 1179648
